TPU v7x, 256 devices: a whole 4x4x8 slice. The times are simulated.
256 devices in a mesh: dp: 16 (over y, x), tensor: 16 (over z, core).
Axes of the slice: x: 4, y: 4, z: 8, core: 2. Of those that a mesh axis runs over, the one named last changes fastest.
Arguments:
- grad_up: bfloat16 [32768, 28672], P('dp', 'tensor'), may hold values from -240 to 240
- activations: bfloat16 [32768, 8192], P('dp', 'tensor'), may hold values from -6 to 6
- segment_ids: int32 [16, 2048], P('dp'), may hold values from 0 to 15, never falling along the last dimension, each value on 1 to 256 neighbouring positions
- proj_out: bfloat16 [64, 28672], P(None, 'tensor'), may hold values from -0.09449112 to 0.09449112
- proj_in: bfloat16 [64, 8192], P(None, 'tensor'), may hold values from -0.0625 to 0.0625
Outputs:
- fisher: float32 [4096, 4096], P('tensor', 'dp')
Inputs may be any that keep to these rules, and one draw needn't show every extreme that they name: `segment_ids`: each row numbers its tokens' examples 0 to 15 in order, never falling; every example has 1 to 256 tokens, and one has exactly 256.
All inputs are finite; a program needn't handle non-finite values.
Results may differ from a plain program's by a relative error of at most 0.0003.
Values sent between devices are 32-bit elements; how exact they have to be, the bound alone decides.
A program may use at most 64 MiB of HBM per device.

v0:
```python
import jax
import jax.numpy as jnp
from jax import lax
from jax.sharding import PartitionSpec as P

E_DEV = 16


def segment_outer(token_proj, segment_row, examples, proj_width):
    out_proj = token_proj[:, :proj_width]
    in_proj = token_proj[:, proj_width:]
    member = (segment_row[:, None] == jnp.arange(examples, dtype=jnp.int32)[None, :]).astype(
        jnp.float32
    )
    weighted = (member[:, :, None] * out_proj[:, None, :]).reshape(
        token_proj.shape[0], examples * proj_width
    )
    blocked = lax.dot_general(
        weighted,
        in_proj,
        (((0,), (0,)), ((), ())),
        precision=lax.Precision.HIGHEST,
        preferred_element_type=jnp.float32,
    )
    return blocked.reshape(examples, proj_width * proj_width)


def shards(grad_up, activations, segment_ids, proj_out, proj_in):
    proj_width = proj_out.shape[0]
    square = proj_width * proj_width
    examples = E_DEV
    contract_last = (((1,), (1,)), ((), ()))
    partial_proj = jnp.concatenate(
        [
            lax.dot_general(grad_up, proj_out, contract_last, preferred_element_type=jnp.float32),
            lax.dot_general(
                activations, proj_in, contract_last, preferred_element_type=jnp.float32
            ),
        ],
        axis=1,
    )
    segment_row = segment_ids[0]
    summed_proj = lax.psum(partial_proj, "tensor")
    per_example = segment_outer(summed_proj, segment_row, examples, proj_width)
    column_part = lax.all_to_all(per_example, "dp", split_axis=1, concat_axis=0, tiled=True)
    row_width = square // lax.axis_size("tensor")
    own_rows = lax.dynamic_slice_in_dim(
        per_example, lax.axis_index("tensor") * row_width, row_width, 1
    )
    raw_fisher = lax.dot_general(
        lax.all_gather(own_rows, "dp", axis=0, tiled=True),
        column_part,
        (((0,), (0,)), ((), ())),
        precision=lax.Precision.HIGHEST,
        preferred_element_type=jnp.float32,
    )
    trace = lax.psum(jnp.sum(column_part * column_part), "dp")
    return raw_fisher / (trace / square + 1e-06)


def solution(mesh):
    in_specs = (
        P("dp", "tensor"),
        P("dp", "tensor"),
        P("dp", None),
        P(None, "tensor"),
        P(None, "tensor"),
    )
    out_specs = P("tensor", "dp")
    return jax.shard_map(shards, mesh=mesh, in_specs=in_specs, out_specs=out_specs, check_vma=False)
```

profile of v0, /device:TPU:96, one launch (start us, length us, event | category | flops | bytes accessed | tf_op | source)
XLA Modules:
  0.0 224.9 jit_solution(11616446983103335068)
XLA Ops:
  6.5 0.0 copy-start
  6.5 0.0 copy-start.2
  6.5 0.0 all-reduce.2.cloned.1.call-start
  6.5 1.6 copy-done
  8.1 1.6 fusion.5
  9.7 5.4 %fusion.4 = f32[2048,64]{0,1:T(8,128)S(1)} fusion(bf16[2048,1792]{1,0:T(8,128)(2,1)} %param.5, bf16[64,1792]{1,0:T(8,128)(2,1)} %param.8), kind=kOutput, calls=%fused_computation.10 | convolution fusion | flops 469762048 | bytes 8093696 | tf_op jit(solution)/shard_map/dot_general | solution.py:35
  15.1 1.1 pad_maximum_fusion
  16.2 0.0 all-reduce.2.cloned.1.call-update
  16.3 0.0 copy-done.2
  16.3 112.3 %all-reduce.2.cloned.1.call-done = f32[2048,128]{0,1:T(8,128)} async-done(((f32[2048,128]{0,1:T(8,128)}), f32[2048,128]{0,1:T(8,128)}) %all-reduce.2.cloned.1.call-update) | async-done | bytes 1048592 | tf_op jit(solution)/shard_map/psum | solution.py:43
  128.6 0.0 copy-start.1
  128.6 1.2 slice.8
  129.8 1.1 broadcast_multiply_fusion
  130.8 0.0 copy-done.1
  130.8 6.6 %fusion = f32[1024,64]{1,0:T(8,128)S(1)} fusion(f32[2048,1024]{0,1:T(8,128)S(1)} %bitcast.15, f32[2048,128]{0,1:T(8,128)S(1)} %copy-done.1), kind=kOutput, calls=%fused_computation.3 | convolution fusion | flops 1610612736 | bytes 9175040 | tf_op jit(solution)/shard_map/dot_general | solution.py:18
  137.5 0.2 all_to_all.14
  137.6 0.9 copy.12
  138.5 6.8 %all-to-all-start = ((f32[16,16,256]{2,0,1:T(8,128)}), f32[16,16,256]{2,0,1:T(8,128)S(1)}, u32[]{:S(2)}, u32[]{:S(2)}) async-start(f32[16,16,256]{2,0,1:T(8,128)} %copy.12), calls=%async_computation | async-start | bytes 524288 | tf_op jit(solution)/shard_map/all_to_all | solution.py:45
  145.3 0.2 reshape.37
  145.5 9.6 %all-to-all-done = f32[16,16,256]{2,0,1:T(8,128)S(1)} async-done(((f32[16,16,256]{2,0,1:T(8,128)}), f32[16,16,256]{2,0,1:T(8,128)S(1)}, u32[]{:S(2)}, u32[]{:S(2)}) %all-to-all-start) | async-done | bytes 262176 | tf_op jit(solution)/shard_map/all_to_all | solution.py:45
  155.1 0.7 fusion.2
  155.8 21.5 %all_gather.3 = f32[256,256]{1,0:T(8,128)S(1)} all-gather(f32[16,256]{1,0:T(8,128)S(1)} %constant_dynamic-slice_fusion), channel_id=1, replica_groups=mesh['dp'=16,'tensor'=16] {'dp'}, dimensions={0}, use_global_device_ids=true | all-gather | bytes 278528 | tf_op jit(solution)/shard_map/all_gather | solution.py:51
  177.3 38.8 %psum.15 = f32[]{:T(128)} all-reduce(f32[]{:T(128)} %fusion.2), channel_id=1, replica_groups=mesh['dp'=16,'tensor'=16] {'dp'}, use_global_device_ids=true, to_apply=%region_2.0 | all-reduce | flops 1 | bytes 8 | tf_op jit(solution)/shard_map/psum | solution.py:57
  216.7 1.3 convolution_divide_fusion
  (2 shorter events, 0.0 us)
Async XLA Ops:
  6.5 1.6 copy-start
  6.5 9.7 %copy-start.2 = (s32[1,2048]{1,0:T(1,128)S(1)}, s32[1,2048]{1,0:T(1,128)}, u32[]{:S(2)}) copy-start(s32[1,2048]{1,0:T(1,128)} %param.7) | copy-start | bytes 24580
  6.5 122.0 %all-reduce.2.cloned.1.call-start = ((), (), s32[]{:S(2)}) async-start(), calls=%async_computation.1 | async-start | bytes 2097152 | tf_op jit(solution)/shard_map/psum | solution.py:43
  128.6 2.2 copy-start.1
  138.5 16.6 %all-to-all-start = ((f32[16,16,256]{2,0,1:T(8,128)}), f32[16,16,256]{2,0,1:T(8,128)S(1)}, u32[]{:S(2)}, u32[]{:S(2)}) async-start(f32[16,16,256]{2,0,1:T(8,128)} %copy.12), calls=%async_computation | async-start | bytes 524288 | tf_op jit(solution)/shard_map/all_to_all | solution.py:45
Sparse Core Ops, SparseCore 0:
  16.4 112.1 all-reduce.1
where the time goes:
time: 225 us
  waiting for transfers between devices  122 us (54%)
  blocking collectives  60.3 us (27%)
  matrix products  14.9 us (7%)
  between operations  14.1 us (6%)
  starting transfers between devices  6.81 us (3%)
  local copies, waits for them, and re-layouts  3.98 us (2%)
  other arithmetic  2.86 us (1%)
    psum x1, waiting for transfers between devices, shards(): summed_proj = lax.psum(partial_proj, 'tensor')  112 us
    psum x1, blocking collectives, shards(): trace = lax.psum(jnp.sum(column_part * column_part), 'dp')  38.8 us
    all_gather x1, blocking collectives, shards(): lax.all_gather(own_rows, 'dp', axis=0, tiled=True)  21.5 us
    all_to_all x1, waiting for transfers between devices, shards(): lax.all_to_all(per_example, 'dp', split_axis=1, concat_axis=0, tiled=True)  9.56 us
    all_to_all x1, starting transfers between devices, shards(): lax.all_to_all(per_example, 'dp', split_axis=1, concat_axis=0, tiled=True)  6.81 us
    dot_general x1, matrix products, segment_outer(): lax.dot_general(weighted, in_proj, (((0,), (0,)), ((), ())), precision=la...  6.63 us
    dot_general x1, matrix products, shards(): lax.dot_general(grad_up, proj_out, contract_last, preferred_element_type=...  5.4 us
  transfers between devices with their start and end apart: 2, of which 2 were waited for; matrix products, arithmetic and copies ran while one was open for 0% of the time, Pallas kernels for 0%

commit v1 on v0

v1 whole, which is shorter than its diff:
```python
import functools

import jax
import jax.numpy as jnp
from jax import lax
from jax.experimental import pallas as pl
from jax.experimental.pallas import tpu as pltpu
from jax.sharding import PartitionSpec as P

MESH = pl.DeviceIdType.MESH
F32 = jnp.float32
BF16 = jnp.bfloat16
EXAMPLES = 16
PROJ = 64
LANES = 128


def split(x):
    high = x.astype(BF16)
    low = (x - high.astype(F32)).astype(BF16)
    return high, low


def order(i):
    return 4 - (i + 1) // 2 if i % 2 else 4 + i // 2


def kernel(
    ndp, nz, nt,
    grad_hbm, act_hbm, seg_hbm, po_hbm, pi_hbm, out_ref,
    gbuf, abuf, seg, wout, win, part, sib_recv, rs_send, rs_recv, tok,
    high_ref, low_ref, xacc, xs_recv, xd, msg, rows, cols, ss, ss_recv,
    g_sem, a_sem, w_sem, sib_s, sib_r, rs_s, rs_r, ag_s, ag_r, xs_sem,
    row_s, row_r, col_s, col_r, fw_s, fw_r, ss_sem,
):
    d = lax.axis_index("dp")
    t = lax.axis_index("tensor")
    z, c = t // 2, t % 2
    sibling = (d, t + 1 - 2 * c)
    chunk = 2 * nt

    def zdev(k):
        return (d, ((z + k) % nz) * 2 + c)

    def remote(src, dst, send, recv, device):
        return pltpu.make_async_remote_copy(
            src_ref=src, dst_ref=dst, send_sem=send, recv_sem=recv,
            device_id=device, device_id_type=MESH,
        )

    barrier = pltpu.get_barrier_semaphore()
    for k in range(1, nz):
        pl.semaphore_signal(barrier, inc=1, device_id=zdev(k), device_id_type=MESH)
    for k in range(1, ndp):
        pl.semaphore_signal(barrier, inc=1, device_id=((d + k) % ndp, t), device_id_type=MESH)
    pl.semaphore_signal(barrier, inc=1, device_id=sibling, device_id_type=MESH)

    weights = [
        pltpu.make_async_copy(po_hbm, wout.at[pl.ds(0, PROJ)], w_sem.at[0]),
        pltpu.make_async_copy(pi_hbm, win.at[pl.ds(PROJ, PROJ)], w_sem.at[1]),
        pltpu.make_async_copy(seg_hbm, seg, w_sem.at[2]),
    ]
    for copy in weights:
        copy.start()
    loads = []
    for i in range(nz):
        first = pl.multiple_of(((z + order(i)) % nz) * chunk, chunk)
        loads.append((
            pltpu.make_async_copy(grad_hbm.at[pl.ds(first, chunk)], gbuf.at[i], g_sem.at[i]),
            pltpu.make_async_copy(act_hbm.at[pl.ds(first, chunk)], abuf.at[i], a_sem.at[i]),
        ))
        loads[-1][0].start()
        loads[-1][1].start()

    wout[pl.ds(PROJ, PROJ)] = jnp.zeros((PROJ, wout.shape[1]), BF16)
    win[pl.ds(0, PROJ)] = jnp.zeros((PROJ, win.shape[1]), BF16)
    xacc[...] = jnp.zeros_like(xacc)
    for copy in weights:
        copy.wait()

    last = (((1,), (1,)), ((), ()))
    for i in range(nz):
        loads[i][0].wait()
        loads[i][1].wait()
        summed = lax.dot_general(gbuf[i], wout[...], last, preferred_element_type=F32)
        summed += lax.dot_general(abuf[i], win[...], last, preferred_element_type=F32)
        part[i] = summed.reshape(2, nt, LANES)

    pl.semaphore_wait(barrier, nz - 1 + ndp - 1 + 1)

    sib = [
        remote(part.at[i, 1 - c], sib_recv.at[i], sib_s.at[i], sib_r.at[i], sibling)
        for i in range(nz)
    ]
    for copy in sib:
        copy.start()
    scatter = [
        remote(rs_send.at[i], rs_recv.at[i], rs_s.at[i], rs_r.at[i], zdev(order(i)))
        for i in range(nz - 1)
    ]
    for i in range(nz):
        sib[i].wait_recv()
        rs_send[i] = part[i, c] + sib_recv[i]
        if i < nz - 1:
            scatter[i].start()
    total = rs_send[nz - 1]
    for i in range(nz - 1):
        scatter[i].wait_recv()
        total += rs_recv[i]
    tok[z] = total
    gather = [
        remote(tok.at[z], tok.at[z], ag_s.at[i], ag_r.at[z], zdev(order(i)))
        for i in range(nz - 1)
    ]
    for copy in gather:
        copy.start()

    lane = lax.broadcasted_iota(jnp.int32, (nt, LANES), 1)
    example = lax.broadcasted_iota(jnp.int32, (EXAMPLES, nt), 0)

    def accumulate(owner):
        sums = tok[owner]
        flipped = sums.T
        high = flipped[:PROJ].astype(BF16).astype(F32)
        high_ref[...] = high
        low_ref[...] = flipped[:PROJ] - high
        first = pl.multiple_of(owner * chunk + c * nt, nt)
        member = seg[:, pl.ds(first, nt)] == example
        even = jnp.where(lane < PROJ, pltpu.roll(sums, PROJ, 1), 0.0)
        odd = jnp.where(lane < PROJ, 0.0, sums)
        in_high, in_low = split(jnp.concatenate([even, odd], axis=0))
        both = jnp.concatenate([in_high, in_low], axis=1)

        def weigh(ref, p):
            pair = [
                jnp.where(member, jnp.broadcast_to(ref[pl.ds(p + parity, 1), :], member.shape), 0.0)
                for parity in range(2)
            ]
            return jnp.concatenate(pair, axis=1).astype(BF16)

        for half in range(2):
            for quarter in range(4):
                ps = [
                    8 * zz + 4 * half + 2 * jj
                    for zz in (2 * quarter, 2 * quarter + 1) for jj in range(2)
                ]
                w_high = jnp.concatenate([weigh(high_ref, p) for p in ps], axis=0)
                w_low = jnp.concatenate([weigh(low_ref, p) for p in ps], axis=0)
                one = jnp.dot(w_high, both, preferred_element_type=F32)
                two = jnp.dot(w_low, in_high, preferred_element_type=F32)
                block = one[:, :LANES] + (one[:, LANES:] + two)
                xacc[half, pl.ds(2 * quarter, 2)] += block.reshape(2, 2 * EXAMPLES, LANES)

    accumulate(z)
    for i in range(nz - 1):
        owner = (z - order(i) + nz) % nz
        remote(tok.at[z], tok.at[owner], ag_s.at[i], ag_r.at[owner], zdev(order(i))).wait_recv()
        accumulate(owner)

    swap = remote(xacc.at[1 - c], xs_recv, xs_sem.at[0], xs_sem.at[1], sibling)
    swap.start()
    swap.wait_recv()
    mine = xacc[c] + xs_recv[...]
    xd[...] = mine
    msg[pl.ds(0, 2 * EXAMPLES)] = xd[z]
    msg[pl.ds(2 * EXAMPLES, 8)] = jnp.sum((mine * mine).reshape(-1, 8, LANES), axis=0)

    home = d // 2
    forwards = c == d % 2

    def column(m):
        place = (home + m) % (ndp // 2)
        return remote(
            xd.at[place], cols.at[d], col_s.at[m], col_r.at[d], (2 * place + c, t)
        )

    def column_from(source):
        return remote(xd.at[0], cols.at[source], col_s.at[0], col_r.at[source], (source, t))

    def forward(source):
        return remote(cols.at[source], cols.at[source], fw_s.at[source], fw_r.at[source], sibling)

    def row(k):
        return remote(msg, rows.at[d], row_s.at[k], row_r.at[d], ((d + k) % ndp, t))

    def row_from(source):
        return remote(msg, rows.at[source], row_s.at[1], row_r.at[source], (source, t))

    for m in range(1, ndp // 2):
        column(m).start()

    @pl.when(jnp.logical_not(forwards))
    def _():
        column(0).start()

    for k in range(1, ndp):
        row(k).start()
    rows[d] = msg[...]

    @pl.when(forwards)
    def _():
        cols[d] = xd[home]
        forward(d).start()
        for k in range(1, ndp):
            source = (d + k) % ndp
            column_from(source).wait_recv()
            forward(source).start()

    for k in range(1, ndp):
        row_from((d + k) % ndp).wait_recv()
    ss[...] = jnp.sum(rows[:, pl.ds(2 * EXAMPLES, 8), :], axis=0)
    swap_ss = remote(ss, ss_recv, ss_sem.at[0], ss_sem.at[1], sibling)
    swap_ss.start()

    def matrix(ref):
        return jnp.concatenate(
            [
                ref[:, pl.ds(jj * EXAMPLES, EXAMPLES), :].reshape(ndp * EXAMPLES, LANES)
                for jj in range(2)
            ],
            axis=1,
        )

    left_high, left_low = split(matrix(rows).T)

    @pl.when(jnp.logical_not(forwards))
    def _():
        for k in range(ndp):
            forward((d + k) % ndp).wait_recv()

    right_high, right_low = split(matrix(cols))
    swap_ss.wait_recv()
    trace = jnp.sum(ss[...] + ss_recv[...])
    scale = 1.0 / (trace / (PROJ * PROJ) + 1e-6)
    raw = jnp.dot(left_high, right_high, preferred_element_type=F32)
    raw += jnp.dot(left_high, right_low, preferred_element_type=F32)
    raw += jnp.dot(left_low, right_high, preferred_element_type=F32)
    out_ref[...] = raw * scale

    for copy in sib + scatter + gather + [swap, swap_ss]:
        copy.wait_send()
    for m in range(1, ndp // 2):
        column(m).wait_send()
    for k in range(1, ndp):
        row(k).wait_send()

    @pl.when(forwards)
    def _():
        for k in range(ndp):
            forward(k).wait_send()

    @pl.when(jnp.logical_not(forwards))
    def _():
        column(0).wait_send()


def shards(ndp, nz, grad_up, activations, segment_ids, proj_out, proj_in):
    tokens, hidden = grad_up.shape
    features = activations.shape[1]
    nt = tokens // (2 * nz)
    rows = 2 * EXAMPLES
    dma = pltpu.SemaphoreType.DMA
    return pl.pallas_call(
        functools.partial(kernel, ndp, nz, nt),
        out_shape=jax.ShapeDtypeStruct((4 * PROJ, 4 * PROJ), F32),
        in_specs=[pl.BlockSpec(memory_space=pl.ANY)] * 5,
        out_specs=pl.BlockSpec(memory_space=pltpu.VMEM),
        scratch_shapes=[
            pltpu.VMEM((nz, 2 * nt, hidden), BF16),
            pltpu.VMEM((nz, 2 * nt, features), BF16),
            pltpu.VMEM((1, tokens), jnp.int32),
            pltpu.VMEM((2 * PROJ, hidden), BF16),
            pltpu.VMEM((2 * PROJ, features), BF16),
            pltpu.VMEM((nz, 2, nt, LANES), F32),
            pltpu.VMEM((nz, nt, LANES), F32),
            pltpu.VMEM((nz, nt, LANES), F32),
            pltpu.VMEM((nz, nt, LANES), F32),
            pltpu.VMEM((nz, nt, LANES), F32),
            pltpu.VMEM((PROJ, nt), F32),
            pltpu.VMEM((PROJ, nt), F32),
            pltpu.VMEM((2, nz, rows, LANES), F32),
            pltpu.VMEM((nz, rows, LANES), F32),
            pltpu.VMEM((nz, rows, LANES), F32),
            pltpu.VMEM((rows + 8, LANES), F32),
            pltpu.VMEM((ndp, rows + 8, LANES), F32),
            pltpu.VMEM((ndp, rows, LANES), F32),
            pltpu.VMEM((8, LANES), F32),
            pltpu.VMEM((8, LANES), F32),
            dma((nz,)), dma((nz,)), dma((3,)),
            dma((nz,)), dma((nz,)), dma((nz,)), dma((nz,)), dma((nz,)), dma((nz,)), dma((2,)),
            dma((ndp,)), dma((ndp,)), dma((ndp,)), dma((ndp,)), dma((ndp,)), dma((ndp,)), dma((2,)),
        ],
        compiler_params=pltpu.CompilerParams(
            collective_id=0, has_side_effects=True, vmem_limit_bytes=56 * 2**20
        ),
        cost_estimate=pl.CostEstimate(
            flops=2 * tokens * (hidden + features) * PROJ,
            bytes_accessed=2 * tokens * (hidden + features),
            transcendentals=0,
        ),
    )(grad_up, activations, segment_ids, proj_out, proj_in)


def solution(mesh):
    in_specs = (
        P("dp", "tensor"),
        P("dp", "tensor"),
        P("dp", None),
        P(None, "tensor"),
        P(None, "tensor"),
    )
    body = functools.partial(shards, mesh.shape["dp"], mesh.shape["tensor"] // 2)
    return jax.shard_map(
        body, mesh=mesh, in_specs=in_specs, out_specs=P("tensor", "dp"), check_vma=False
    )
```

time: 225 us -> 60.2 us (0.27)
  the two profiles are of different devices: /device:TPU:96 before, /device:TPU:1 now
where the time goes in v1:
time: 60.2 us; the launch traced here: 60.1 us
  Pallas kernels  58.4 us (97%)
  local copies, waits for them, and re-layouts  1.67 us (3%)
    pallas_call x1, Pallas kernels, shards(): pl.pallas_call(functools.partial(kernel, ndp, nz, nt), out_shape=jax.Shap...  58.4 us
    unnamed x1, local copies, waits for them, and re-layouts  1.67 us

profile of v1, /device:TPU:1, one launch (start us, length us, event | category | flops | bytes accessed | tf_op | source)
XLA Modules:
  0.0 60.1 jit_solution(15117433661726810926)
XLA Ops:
  0.0 58.4 %shard_map.55 = f32[256,256]{1,0:T(8,128)} custom-call(bf16[2048,1792]{1,0:T(8,128)(2,1)} %grad_hbm.1, bf16[2048,512]{1,0:T(8,128)(2,1)} %act_hbm.1, s32[1,2048]{1,0:T(1,128)} %seg_hbm.1, bf16[64,1792]{1,0:T(8,128)(2,1)} %po_hbm.1, bf16[64,512]{1,0:T(8,128)(2,1)} %pi_hbm.1), custom_call_target="tpu_custom_call" | custom-call | flops 603979776 | bytes 9437184 | tf_op jit(solution)/shard_map/pallas_call | solution.py:263
  58.4 1.7 %copy.7 = f32[256,256]{1,0:T(8,128)} copy(f32[256,256]{1,0:T(8,128)} %shard_map.55) | data formatting | bytes 524288

commit v2 on v1

--- a/solution.py
+++ b/solution.py
@@ -27,11 +27,11 @@
 
 def kernel(
     ndp, nz, nt,
-    grad_hbm, act_hbm, seg_hbm, po_hbm, pi_hbm, out_ref,
-    gbuf, abuf, seg, wout, win, part, sib_recv, rs_send, rs_recv, tok,
+    grad_hbm, act_hbm, seg_hbm, po_hbm, pi_hbm, left_ref, right_ref, scale_ref,
+    gbuf, abuf, seg, wout, win, wt_out, wt_in, part, sib_recv, sums, far_recv, near_recv, tok,
     high_ref, low_ref, xacc, xs_recv, xd, msg, rows, cols, ss, ss_recv,
-    g_sem, a_sem, w_sem, sib_s, sib_r, rs_s, rs_r, ag_s, ag_r, xs_sem,
-    row_s, row_r, col_s, col_r, fw_s, fw_r, ss_sem,
+    g_sem, a_sem, w_sem, sib_s, sib_r, far_s, far_r, near_s, near_r, ag_s, ag_r, fa_s, fa_r,
+    xs_sem, row_s, row_r, col_s, col_r, fw_s, fw_r, ss_sem,
 ):
     d = lax.axis_index("dp")
     t = lax.axis_index("tensor")
@@ -40,7 +40,7 @@
     chunk = 2 * nt
 
     def zdev(k):
-        return (d, ((z + k) % nz) * 2 + c)
+        return (d, ((z + k + nz) % nz) * 2 + c)
 
     def remote(src, dst, send, recv, device):
         return pltpu.make_async_remote_copy(
@@ -49,7 +49,7 @@
         )
 
     barrier = pltpu.get_barrier_semaphore()
-    for k in range(1, nz):
+    for k in (1, -1, 2, -2):
         pl.semaphore_signal(barrier, inc=1, device_id=zdev(k), device_id_type=MESH)
     for k in range(1, ndp):
         pl.semaphore_signal(barrier, inc=1, device_id=((d + k) % ndp, t), device_id_type=MESH)
@@ -77,57 +77,123 @@
     xacc[...] = jnp.zeros_like(xacc)
     for copy in weights:
         copy.wait()
-
-    last = (((1,), (1,)), ((), ()))
-    for i in range(nz):
+    wt_out[...] = wout[...].T
+    wt_in[...] = win[...].T
+
+    def project(i):
         loads[i][0].wait()
         loads[i][1].wait()
-        summed = lax.dot_general(gbuf[i], wout[...], last, preferred_element_type=F32)
-        summed += lax.dot_general(abuf[i], win[...], last, preferred_element_type=F32)
-        part[i] = summed.reshape(2, nt, LANES)
-
-    pl.semaphore_wait(barrier, nz - 1 + ndp - 1 + 1)
+        for h in range(2):
+            at = pl.ds(h * nt, nt)
+            both = jnp.dot(gbuf[i, at], wt_out[...], preferred_element_type=F32)
+            both += jnp.dot(abuf[i, at], wt_in[...], preferred_element_type=F32)
+            part[i, h] = both.reshape(2, nt // 2, LANES)
+
+    ahead = 3
+    for i in range(ahead):
+        project(i)
+    pl.semaphore_wait(barrier, 4 + ndp - 1 + 1)
 
     sib = [
         remote(part.at[i, 1 - c], sib_recv.at[i], sib_s.at[i], sib_r.at[i], sibling)
         for i in range(nz)
     ]
-    for copy in sib:
-        copy.start()
-    scatter = [
-        remote(rs_send.at[i], rs_recv.at[i], rs_s.at[i], rs_r.at[i], zdev(order(i)))
-        for i in range(nz - 1)
-    ]
+    at = {order(i) - nz if order(i) > 4 else order(i): i for i in range(nz)}
+    sides = (1, -1)
+
+    def far(s, h):
+        n = 2 * s + h
+        return remote(
+            sums.at[at[3 * sides[s]], h], far_recv.at[s, h], far_s.at[n], far_r.at[n], zdev(sides[s])
+        )
+
+    def farthest(s):
+        return remote(
+            sums.at[at[4], s], far_recv.at[2, s], far_s.at[4 + s], far_r.at[4 + s], zdev(2 * sides[s])
+        )
+
+    def near(s):
+        return remote(sums.at[at[sides[s]]], near_recv.at[s], near_s.at[s], near_r.at[s], zdev(sides[s]))
+
+    def second(s, h):
+        n = 2 + 2 * s + h
+        return remote(
+            sums.at[at[2 * sides[s]], h], near_recv.at[2 + s, h], near_s.at[n], near_r.at[n],
+            zdev(2 * sides[s]),
+        )
+
+    for i in range(ahead):
+        sib[i].start()
     for i in range(nz):
+        if i + ahead < nz:
+            project(i + ahead)
+            sib[i + ahead].start()
         sib[i].wait_recv()
-        rs_send[i] = part[i, c] + sib_recv[i]
-        if i < nz - 1:
-            scatter[i].start()
-    total = rs_send[nz - 1]
-    for i in range(nz - 1):
-        scatter[i].wait_recv()
-        total += rs_recv[i]
-    tok[z] = total
-    gather = [
-        remote(tok.at[z], tok.at[z], ag_s.at[i], ag_r.at[z], zdev(order(i)))
-        for i in range(nz - 1)
-    ]
-    for copy in gather:
-        copy.start()
+        sums[i] = part[i, c] + sib_recv[i]
+        if i == at[4]:
+            farthest(0).start()
+            farthest(1).start()
+        for s in range(2):
+            if i == at[3 * sides[s]]:
+                far(s, 1 - s).start()
+                far(s, s).start()
+            if i == at[sides[s]]:
+                near(s).start()
+    for s in range(2):
+        far(s, 1 - s).wait_recv()
+        sums[at[2 * sides[s]], 1 - s] += far_recv[s, 1 - s]
+        second(s, 1 - s).start()
+    for s in range(2):
+        far(s, s).wait_recv()
+        farthest(s).wait_recv()
+        sums[at[2 * sides[s]], s] += far_recv[s, s] + far_recv[2, s]
+        second(s, s).start()
+    for s in range(2):
+        near(s).wait_recv()
+    tok[z] = sums[at[0]] + (near_recv[0] + near_recv[1])
+    for h in range(2):
+        second(0, h).wait_recv()
+        second(1, h).wait_recv()
+        tok[z, h] += near_recv[2, h] + near_recv[3, h]
+
+    def owner(k):
+        return (z + k + nz) % nz
+
+    def spread(s, h):
+        n = 2 * s + h
+        return remote(tok.at[z, h], tok.at[z, h], ag_s.at[n], ag_r.at[n], zdev(2 * sides[s]))
+
+    def beside(s):
+        return remote(tok.at[z], tok.at[z], ag_s.at[4 + s], ag_r.at[4 + s], zdev(sides[s]))
+
+    def onward(s, h):
+        n = 2 * s + h
+        mine = tok.at[owner(-2 * sides[s]), h]
+        return remote(mine, mine, fa_s.at[n], fa_r.at[n], zdev(sides[s]))
+
+    def opposite(s):
+        mine = tok.at[owner(-2 * sides[s]), s]
+        return remote(mine, mine, fa_s.at[4 + s], fa_r.at[4 + s], zdev(2 * sides[s]))
+
+    for first in range(2):
+        for s in range(2):
+            spread(s, s if first == 0 else 1 - s).start()
+    for s in range(2):
+        beside(s).start()
 
     lane = lax.broadcasted_iota(jnp.int32, (nt, LANES), 1)
     example = lax.broadcasted_iota(jnp.int32, (EXAMPLES, nt), 0)
 
-    def accumulate(owner):
-        sums = tok[owner]
-        flipped = sums.T
+    def accumulate(chip):
+        whole = tok[chip].reshape(nt, LANES)
+        flipped = whole.T
         high = flipped[:PROJ].astype(BF16).astype(F32)
         high_ref[...] = high
         low_ref[...] = flipped[:PROJ] - high
-        first = pl.multiple_of(owner * chunk + c * nt, nt)
+        first = pl.multiple_of(chip * chunk + c * nt, nt)
         member = seg[:, pl.ds(first, nt)] == example
-        even = jnp.where(lane < PROJ, pltpu.roll(sums, PROJ, 1), 0.0)
-        odd = jnp.where(lane < PROJ, 0.0, sums)
+        even = jnp.where(lane < PROJ, pltpu.roll(whole, PROJ, 1), 0.0)
+        odd = jnp.where(lane < PROJ, 0.0, whole)
         in_high, in_low = split(jnp.concatenate([even, odd], axis=0))
         both = jnp.concatenate([in_high, in_low], axis=1)
 
@@ -152,10 +218,25 @@
                 xacc[half, pl.ds(2 * quarter, 2)] += block.reshape(2, 2 * EXAMPLES, LANES)
 
     accumulate(z)
-    for i in range(nz - 1):
-        owner = (z - order(i) + nz) % nz
-        remote(tok.at[z], tok.at[owner], ag_s.at[i], ag_r.at[owner], zdev(order(i))).wait_recv()
-        accumulate(owner)
+    for s in range(2):
+        spread(s, s).wait_recv()
+        opposite(s).start()
+        onward(s, s).start()
+    for s in range(2):
+        spread(s, 1 - s).wait_recv()
+        onward(s, 1 - s).start()
+    for s in range(2):
+        accumulate(owner(-2 * sides[s]))
+    for s in range(2):
+        beside(s).wait_recv()
+        accumulate(owner(-sides[s]))
+    for s in range(2):
+        for h in range(2):
+            onward(s, h).wait_recv()
+        accumulate(owner(-3 * sides[s]))
+    for s in range(2):
+        opposite(s).wait_recv()
+    accumulate(owner(4))
 
     swap = remote(xacc.at[1 - c], xs_recv, xs_sem.at[0], xs_sem.at[1], sibling)
     swap.start()
@@ -212,33 +293,32 @@
     swap_ss = remote(ss, ss_recv, ss_sem.at[0], ss_sem.at[1], sibling)
     swap_ss.start()
 
-    def matrix(ref):
-        return jnp.concatenate(
-            [
-                ref[:, pl.ds(jj * EXAMPLES, EXAMPLES), :].reshape(ndp * EXAMPLES, LANES)
-                for jj in range(2)
-            ],
-            axis=1,
-        )
-
-    left_high, left_low = split(matrix(rows).T)
+    def matrix(ref, out):
+        for jj in range(2):
+            out[:, pl.ds(jj * LANES, LANES)] = ref[:, pl.ds(jj * EXAMPLES, EXAMPLES), :].reshape(
+                ndp * EXAMPLES, LANES
+            )
+
+    matrix(rows, left_ref)
 
     @pl.when(jnp.logical_not(forwards))
     def _():
         for k in range(ndp):
             forward((d + k) % ndp).wait_recv()
 
-    right_high, right_low = split(matrix(cols))
+    matrix(cols, right_ref)
     swap_ss.wait_recv()
-    trace = jnp.sum(ss[...] + ss_recv[...])
-    scale = 1.0 / (trace / (PROJ * PROJ) + 1e-6)
-    raw = jnp.dot(left_high, right_high, preferred_element_type=F32)
-    raw += jnp.dot(left_high, right_low, preferred_element_type=F32)
-    raw += jnp.dot(left_low, right_high, preferred_element_type=F32)
-    out_ref[...] = raw * scale
-
-    for copy in sib + scatter + gather + [swap, swap_ss]:
+    trace = jnp.sum(ss[...] + ss_recv[...], keepdims=True)
+    scale_ref[...] = trace / (PROJ * PROJ) + 1e-6
+
+    for copy in sib + [swap, swap_ss]:
         copy.wait_send()
+    for s in range(2):
+        for copy in (farthest(s), near(s), beside(s), opposite(s)):
+            copy.wait_send()
+        for h in range(2):
+            for copy in (far(s, h), second(s, h), spread(s, h), onward(s, h)):
+                copy.wait_send()
     for m in range(1, ndp // 2):
         column(m).wait_send()
     for k in range(1, ndp):
@@ -259,23 +339,32 @@
     features = activations.shape[1]
     nt = tokens // (2 * nz)
     rows = 2 * EXAMPLES
+    block = 4 * PROJ
     dma = pltpu.SemaphoreType.DMA
-    return pl.pallas_call(
+    halves = (2, nt // 2, LANES)
+    left, right, scale = pl.pallas_call(
         functools.partial(kernel, ndp, nz, nt),
-        out_shape=jax.ShapeDtypeStruct((4 * PROJ, 4 * PROJ), F32),
+        out_shape=[
+            jax.ShapeDtypeStruct((ndp * EXAMPLES, block), F32),
+            jax.ShapeDtypeStruct((ndp * EXAMPLES, block), F32),
+            jax.ShapeDtypeStruct((1, 1), F32),
+        ],
         in_specs=[pl.BlockSpec(memory_space=pl.ANY)] * 5,
-        out_specs=pl.BlockSpec(memory_space=pltpu.VMEM),
+        out_specs=[pl.BlockSpec(memory_space=pltpu.VMEM)] * 3,
         scratch_shapes=[
             pltpu.VMEM((nz, 2 * nt, hidden), BF16),
             pltpu.VMEM((nz, 2 * nt, features), BF16),
             pltpu.VMEM((1, tokens), jnp.int32),
             pltpu.VMEM((2 * PROJ, hidden), BF16),
             pltpu.VMEM((2 * PROJ, features), BF16),
-            pltpu.VMEM((nz, 2, nt, LANES), F32),
-            pltpu.VMEM((nz, nt, LANES), F32),
-            pltpu.VMEM((nz, nt, LANES), F32),
-            pltpu.VMEM((nz, nt, LANES), F32),
-            pltpu.VMEM((nz, nt, LANES), F32),
+            pltpu.VMEM((hidden, 2 * PROJ), BF16),
+            pltpu.VMEM((features, 2 * PROJ), BF16),
+            pltpu.VMEM((nz, 2) + halves, F32),
+            pltpu.VMEM((nz,) + halves, F32),
+            pltpu.VMEM((nz,) + halves, F32),
+            pltpu.VMEM((3,) + halves, F32),
+            pltpu.VMEM((4,) + halves, F32),
+            pltpu.VMEM((nz,) + halves, F32),
             pltpu.VMEM((PROJ, nt), F32),
             pltpu.VMEM((PROJ, nt), F32),
             pltpu.VMEM((2, nz, rows, LANES), F32),
@@ -287,7 +376,8 @@
             pltpu.VMEM((8, LANES), F32),
             pltpu.VMEM((8, LANES), F32),
             dma((nz,)), dma((nz,)), dma((3,)),
-            dma((nz,)), dma((nz,)), dma((nz,)), dma((nz,)), dma((nz,)), dma((nz,)), dma((2,)),
+            dma((nz,)), dma((nz,)), dma((6,)), dma((6,)), dma((6,)), dma((6,)),
+            dma((6,)), dma((6,)), dma((6,)), dma((6,)), dma((2,)),
             dma((ndp,)), dma((ndp,)), dma((ndp,)), dma((ndp,)), dma((ndp,)), dma((ndp,)), dma((2,)),
         ],
         compiler_params=pltpu.CompilerParams(
@@ -299,6 +389,11 @@
             transcendentals=0,
         ),
     )(grad_up, activations, segment_ids, proj_out, proj_in)
+    raw = lax.dot_general(
+        left, right, (((0,), (0,)), ((), ())),
+        precision=lax.Precision.HIGHEST, preferred_element_type=F32,
+    )
+    return raw / scale[0, 0]
 
 
 def solution(mesh):

time: 60.2 us -> 49.1 us (0.82)
  Pallas kernels: 58.4 us -> 46.1 us
  matrix products: 0 us -> 2.9 us
  local copies, waits for them, and re-layouts: 1.67 us -> 0 us
    pallas_call x1, Pallas kernels: 58.4 us -> 46.1 us  [shards(): pl.pallas_call(functools.partial(kernel, ndp, nz, nt), out_shape=[jax.Sha...]
    dot_general x0 -> x1, matrix products: none -> 2.9 us  [shards(): lax.dot_general(left, right, (((0,), (0,)), ((), ())), precision=lax.Prec...]
    unnamed x1 -> x0, local copies, waits for them, and re-layouts: 1.67 us -> none
where the time goes in v2:
time: 49.1 us; the launch traced here: 49 us
  Pallas kernels  46.1 us (94%)
  matrix products  2.9 us (6%)
    pallas_call x1, Pallas kernels, shards(): pl.pallas_call(functools.partial(kernel, ndp, nz, nt), out_shape=[jax.Sha...  46.1 us
    dot_general x1, matrix products, shards(): lax.dot_general(left, right, (((0,), (0,)), ((), ())), precision=lax.Prec...  2.9 us

profile of v2, /device:TPU:1, one launch (start us, length us, event | category | flops | bytes accessed | tf_op | source)
XLA Modules:
  0.0 49.0 jit_solution(9360704755505292800)
XLA Ops:
  0.0 46.1 %shard_map.55 = (f32[256,256]{1,0:T(8,128)}, f32[256,256]{1,0:T(8,128)}, f32[1,1]{1,0:T(1,128)}) custom-call(bf16[2048,1792]{1,0:T(8,128)(2,1)} %grad_hbm.1, bf16[2048,512]{1,0:T(8,128)(2,1)} %act_hbm.1, s32[1,2048]{1,0:T(1,128)} %seg_hbm.1, bf16[64,1792]{1,0:T(8,128)(2,1)} %po_hbm.1, bf16[64,512]{1,0:T(8,128)(2,1)} %pi_hbm.1), custom_call_target="tpu_custom_call" | custom-call | flops 603979776 | bytes 9437184 | tf_op jit(solution)/shard_map/pallas_call | solution.py:345
  46.1 2.9 %convolution_divide_fusion = f32[256,256]{1,0:T(8,128)} fusion(f32[256,256]{1,0:T(8,128)} %get-tuple-element.8, f32[256,256]{1,0:T(8,128)} %get-tuple-element.9, f32[]{:T(128)} %bitcast), kind=kOutput, calls=%fused_computation | convolution fusion | flops 201392128 | bytes 786436 | tf_op jit(solution)/shard_map/dot_general | solution.py:392

commit v3 on v2

v3 whole, which is shorter than its diff:
```python
import functools

import jax
import jax.numpy as jnp
from jax import lax
from jax.experimental import pallas as pl
from jax.experimental.pallas import tpu as pltpu
from jax.sharding import PartitionSpec as P

MESH = pl.DeviceIdType.MESH
F32 = jnp.float32
BF16 = jnp.bfloat16
EXAMPLES = 16
PROJ = 64
LANES = 128
DEPTH = 256
SIDE = 4


def split(x):
    high = x.astype(BF16)
    low = (x - high.astype(F32)).astype(BF16)
    return high, low


def order(i):
    return 4 - (i + 1) // 2 if i % 2 else 4 + i // 2


def kernel(
    ndp, nz, nt,
    grad_hbm, act_hbm, seg_hbm, po_hbm, pi_hbm, left_ref, right_ref, scale_ref,
    gbuf, abuf, seg, wout, win, wt_out, wt_in, part, sib_recv, sums, far_recv, near_recv, tok,
    high_ref, low_ref, xacc, rows, cols, ss, ss_all, ss_sum, ss_recv,
    g_sem, a_sem, w_sem, sib_s, sib_r, far_s, far_r, near_s, near_r, ag_s, ag_r, fa_s, fa_r,
    sh_s, sh_r, row_s, row_r, col_s, col_r, fw_s, fw_r, sq_s, sq_r, ss_sem, ready,
):
    d = lax.axis_index("dp")
    t = lax.axis_index("tensor")
    z, c = lax.div(t, 2), lax.rem(t, 2)
    ring = [lax.rem(z + k, nz) for k in range(nz)]
    plane = [lax.rem(d + k, ndp) for k in range(ndp)]
    sibling = (d, t + 1 - 2 * c)
    chunk = 2 * nt

    def zdev(k):
        return (d, ring[k % nz] * 2 + c)

    def remote(src, dst, send, recv, device):
        return pltpu.make_async_remote_copy(
            src_ref=src, dst_ref=dst, send_sem=send, recv_sem=recv,
            device_id=device, device_id_type=MESH,
        )

    barrier = pltpu.get_barrier_semaphore()
    line = [(lax.div(d, SIDE) * SIDE + lax.rem(d + k, SIDE), t) for k in range(1, SIDE)]
    column_peers = [(plane[SIDE * k], t) for k in range(1, ndp // SIDE)]
    greeted = [zdev(k) for k in (1, -1, 2, -2)] + line + column_peers + [sibling]
    for device in greeted:
        pl.semaphore_signal(barrier, inc=1, device_id=device, device_id_type=MESH)

    weights = [
        pltpu.make_async_copy(po_hbm, wout.at[pl.ds(0, PROJ)], w_sem.at[0]),
        pltpu.make_async_copy(pi_hbm, win.at[pl.ds(PROJ, PROJ)], w_sem.at[1]),
        pltpu.make_async_copy(seg_hbm, seg, w_sem.at[2]),
    ]
    for copy in weights:
        copy.start()
    loads = []
    for i in range(nz):
        first = pl.multiple_of(ring[order(i)] * chunk, chunk)
        loads.append((
            pltpu.make_async_copy(grad_hbm.at[pl.ds(first, chunk)], gbuf.at[i], g_sem.at[i]),
            pltpu.make_async_copy(act_hbm.at[pl.ds(first, chunk)], abuf.at[i], a_sem.at[i]),
        ))
        loads[-1][0].start()
        loads[-1][1].start()

    wout[pl.ds(PROJ, PROJ)] = jnp.zeros((PROJ, wout.shape[1]), BF16)
    win[pl.ds(0, PROJ)] = jnp.zeros((PROJ, win.shape[1]), BF16)
    xacc[...] = jnp.zeros_like(xacc)
    for copy in weights:
        copy.wait()
    wt_out[...] = wout[...].T
    wt_in[...] = win[...].T

    def project(group):
        for i in group:
            loads[i][0].wait()
            loads[i][1].wait()
        total = {}
        for source, weight in ((gbuf, wt_out), (abuf, wt_in)):
            for first in range(0, weight.shape[0], DEPTH):
                for i in group:
                    term = jnp.dot(
                        source[i, :, pl.ds(first, DEPTH)], weight[pl.ds(first, DEPTH)],
                        preferred_element_type=F32,
                    )
                    total[i] = total[i] + term if i in total else term
        for i in group:
            part[i] = total[i].reshape((2, 2, nt // 2, LANES))

    ahead = 3
    project(range(ahead))
    pl.semaphore_wait(barrier, len(greeted))
    for device in line:
        pl.semaphore_signal(ready, inc=1, device_id=device, device_id_type=MESH)

    sib = [
        remote(part.at[i, 1 - c], sib_recv.at[i], sib_s.at[i], sib_r.at[i], sibling)
        for i in range(nz)
    ]
    at = {order(i) - nz if order(i) > 4 else order(i): i for i in range(nz)}
    sides = (1, -1)

    def far(s, h):
        n = 2 * s + h
        return remote(
            sums.at[at[3 * sides[s]], h], far_recv.at[s, h], far_s.at[n], far_r.at[n], zdev(sides[s])
        )

    def farthest(s):
        return remote(
            sums.at[at[4], s], far_recv.at[2, s], far_s.at[4 + s], far_r.at[4 + s], zdev(2 * sides[s])
        )

    def near(s):
        return remote(sums.at[at[sides[s]]], near_recv.at[s], near_s.at[s], near_r.at[s], zdev(sides[s]))

    def second(s, h):
        n = 2 + 2 * s + h
        return remote(
            sums.at[at[2 * sides[s]], h], near_recv.at[2 + s, h], near_s.at[n], near_r.at[n],
            zdev(2 * sides[s]),
        )

    for i in range(ahead):
        sib[i].start()
    groups = {3: (3, 4), 5: (5, 6, 7)}
    for i in range(nz):
        if i in groups:
            project(groups[i])
            for later in groups[i]:
                sib[later].start()
        sib[i].wait_recv()
        sums[i] = part[i, c] + sib_recv[i]
        if i == at[4]:
            farthest(0).start()
            farthest(1).start()
        for s in range(2):
            if i == at[3 * sides[s]]:
                far(s, 1 - s).start()
                far(s, s).start()
            if i == at[sides[s]]:
                near(s).start()
    for s in range(2):
        far(s, 1 - s).wait_recv()
        sums[at[2 * sides[s]], 1 - s] += far_recv[s, 1 - s]
        second(s, 1 - s).start()
    for s in range(2):
        far(s, s).wait_recv()
        farthest(s).wait_recv()
        sums[at[2 * sides[s]], s] += far_recv[s, s] + far_recv[2, s]
        second(s, s).start()
    for s in range(2):
        near(s).wait_recv()
    tok[z, c] = sums[at[0]] + (near_recv[0] + near_recv[1])
    for h in range(2):
        second(0, h).wait_recv()
        second(1, h).wait_recv()
        tok[z, c, h] += near_recv[2, h] + near_recv[3, h]

    def owner(k):
        return ring[k % nz]

    def spread(s, h):
        n = 2 * s + h
        return remote(tok.at[z, c, h], tok.at[z, c, h], ag_s.at[n], ag_r.at[n], zdev(2 * sides[s]))

    def beside(s):
        return remote(tok.at[z, c], tok.at[z, c], ag_s.at[4 + s], ag_r.at[4 + s], zdev(sides[s]))

    def onward(s, h):
        n = 2 * s + h
        mine = tok.at[owner(-2 * sides[s]), c, h]
        return remote(mine, mine, fa_s.at[n], fa_r.at[n], zdev(sides[s]))

    def opposite(s):
        mine = tok.at[owner(-2 * sides[s]), c, s]
        return remote(mine, mine, fa_s.at[4 + s], fa_r.at[4 + s], zdev(2 * sides[s]))

    for first in range(2):
        for s in range(2):
            spread(s, s if first == 0 else 1 - s).start()
    for s in range(2):
        beside(s).start()

    lane = lax.broadcasted_iota(jnp.int32, (nt, LANES), 1)
    example = lax.broadcasted_iota(jnp.int32, (EXAMPLES, nt), 0)

    def share(k):
        mine = tok.at[owner(k), c]
        return remote(mine, mine, sh_s.at[k % nz], sh_r.at[k % nz], sibling)

    def accumulate(k, core):
        chip = owner(k)
        whole = tok[chip, core].reshape(nt, LANES)
        flipped = whole.T
        high = flipped[:PROJ].astype(BF16).astype(F32)
        high_ref[...] = high
        low_ref[...] = flipped[:PROJ] - high
        first = pl.multiple_of(chip * chunk + core * nt, nt)
        member = seg[:, pl.ds(first, nt)] == example
        even = jnp.where(lane < PROJ, pltpu.roll(whole, PROJ, 1), 0.0)
        odd = jnp.where(lane < PROJ, 0.0, whole)
        in_high, in_low = split(jnp.concatenate([even, odd], axis=0))
        both = jnp.concatenate([in_high, in_low], axis=1)

        def weigh(ref, p):
            pair = [
                jnp.where(member, jnp.broadcast_to(ref[pl.ds(p + parity, 1), :], member.shape), 0.0)
                for parity in range(2)
            ]
            return jnp.concatenate(pair, axis=1).astype(BF16)

        for part_of in range(2):
            ps = [8 * zz + 4 * c + 2 * jj for zz in range(4 * part_of, 4 * part_of + 4) for jj in range(2)]
            w_high = jnp.concatenate([weigh(high_ref, p) for p in ps], axis=0)
            w_low = jnp.concatenate([weigh(low_ref, p) for p in ps], axis=0)
            one = jnp.dot(w_high, both, preferred_element_type=F32)
            two = jnp.dot(w_low, in_high, preferred_element_type=F32)
            block = one[:, :LANES] + (one[:, LANES:] + two)
            xacc[pl.ds(4 * part_of, 4)] += block.reshape(4, 2 * EXAMPLES, LANES)

    def own(k):
        accumulate(k, c)

    def others(k):
        share(k).wait_recv()
        accumulate(k, 1 - c)

    share(0).start()
    own(0)
    others(0)
    for s in range(2):
        spread(s, s).wait_recv()
        opposite(s).start()
        onward(s, s).start()
    for s in range(2):
        spread(s, 1 - s).wait_recv()
        onward(s, 1 - s).start()
        share(-2 * sides[s]).start()
    for s in range(2):
        own(-2 * sides[s])
    for s in range(2):
        beside(s).wait_recv()
        share(-sides[s]).start()
    for s in range(2):
        own(-sides[s])
    for s in range(2):
        others(-2 * sides[s])
    for s in range(2):
        others(-sides[s])
    for s in range(2):
        for h in range(2):
            onward(s, h).wait_recv()
        share(-3 * sides[s]).start()
    for s in range(2):
        opposite(s).wait_recv()
    share(4).start()
    for s in range(2):
        own(-3 * sides[s])
    own(4)
    for s in range(2):
        others(-3 * sides[s])
    others(4)

    squares = xacc[...] * xacc[...]
    ss[...] = jnp.sum(squares.reshape(-1, LANES), axis=0, keepdims=True)
    pl.semaphore_wait(ready, len(line))

    home = lax.div(d, 2)
    forwards = c == lax.rem(d, 2)
    places = [lax.rem(home + m, ndp // 2) for m in range(ndp // 2)]

    def column(m):
        place = places[m]
        return remote(
            xacc.at[place], cols.at[d], col_s.at[m], col_r.at[d], (2 * place + c, t)
        )

    def column_from(source):
        return remote(xacc.at[0], cols.at[source], col_s.at[0], col_r.at[source], (source, t))

    def forward(source):
        return remote(cols.at[source], cols.at[source], fw_s.at[source], fw_r.at[source], sibling)

    def row(k):
        return remote(xacc.at[z], rows.at[d], row_s.at[k], row_r.at[d], (plane[k], t))

    def row_from(source):
        return remote(xacc.at[z], rows.at[source], row_s.at[1], row_r.at[source], (source, t))

    def square(k):
        return remote(ss, ss_all.at[d], sq_s.at[k], sq_r.at[d], (plane[k], t))

    def square_from(source):
        return remote(ss, ss_all.at[source], sq_s.at[1], sq_r.at[source], (source, t))

    for m in range(1, ndp // 2):
        column(m).start()

    @pl.when(jnp.logical_not(forwards))
    def _():
        column(0).start()

    for k in range(1, ndp):
        square(k).start()
    for k in range(1, ndp):
        row(k).start()
    rows[d] = xacc[z]
    ss_all[d] = ss[...]

    @pl.when(forwards)
    def _():
        cols[d] = xacc[home]
        forward(d).start()
        for k in range(1, ndp):
            source = plane[k]
            column_from(source).wait_recv()
            forward(source).start()

    for k in range(1, ndp):
        square_from(plane[k]).wait_recv()
    ss_sum[...] = jnp.sum(ss_all[...], axis=0)
    swap_ss = remote(ss_sum, ss_recv, ss_sem.at[0], ss_sem.at[1], sibling)
    swap_ss.start()
    for k in range(1, ndp):
        row_from(plane[k]).wait_recv()

    def matrix(ref, out):
        for jj in range(2):
            out[:, pl.ds(jj * LANES, LANES)] = ref[:, pl.ds(jj * EXAMPLES, EXAMPLES), :].reshape(
                ndp * EXAMPLES, LANES
            )

    matrix(rows, left_ref)

    @pl.when(jnp.logical_not(forwards))
    def _():
        for k in range(ndp):
            forward(plane[k]).wait_recv()

    matrix(cols, right_ref)
    swap_ss.wait_recv()
    trace = jnp.sum(ss_sum[...] + ss_recv[...], keepdims=True)
    scale_ref[...] = trace / (PROJ * PROJ) + 1e-6

    for copy in sib + [swap_ss] + [share(k) for k in range(nz)]:
        copy.wait_send()
    for s in range(2):
        for copy in (farthest(s), near(s), beside(s), opposite(s)):
            copy.wait_send()
        for h in range(2):
            for copy in (far(s, h), second(s, h), spread(s, h), onward(s, h)):
                copy.wait_send()
    for m in range(1, ndp // 2):
        column(m).wait_send()
    for k in range(1, ndp):
        row(k).wait_send()
        square(k).wait_send()

    @pl.when(forwards)
    def _():
        for k in range(ndp):
            forward(k).wait_send()

    @pl.when(jnp.logical_not(forwards))
    def _():
        column(0).wait_send()


def shards(ndp, nz, grad_up, activations, segment_ids, proj_out, proj_in):
    tokens, hidden = grad_up.shape
    features = activations.shape[1]
    nt = tokens // (2 * nz)
    rows = 2 * EXAMPLES
    block = 4 * PROJ
    dma = pltpu.SemaphoreType.DMA
    halves = (2, nt // 2, LANES)
    arrays = (grad_up, activations, segment_ids, proj_out, proj_in)
    in_hbm = [pltpu.with_memory_space_constraint(array, pltpu.HBM) for array in arrays]
    left, right, scale = pl.pallas_call(
        functools.partial(kernel, ndp, nz, nt),
        out_shape=[
            jax.ShapeDtypeStruct((ndp * EXAMPLES, block), F32),
            jax.ShapeDtypeStruct((ndp * EXAMPLES, block), F32),
            jax.ShapeDtypeStruct((1, 1), F32),
        ],
        in_specs=[pl.BlockSpec(memory_space=pltpu.HBM)] * 5,
        out_specs=[pl.BlockSpec(memory_space=pltpu.VMEM)] * 3,
        scratch_shapes=[
            pltpu.VMEM((nz, 2 * nt, hidden), BF16),
            pltpu.VMEM((nz, 2 * nt, features), BF16),
            pltpu.VMEM((1, tokens), jnp.int32),
            pltpu.VMEM((2 * PROJ, hidden), BF16),
            pltpu.VMEM((2 * PROJ, features), BF16),
            pltpu.VMEM((hidden, 2 * PROJ), BF16),
            pltpu.VMEM((features, 2 * PROJ), BF16),
            pltpu.VMEM((nz, 2) + halves, F32),
            pltpu.VMEM((nz,) + halves, F32),
            pltpu.VMEM((nz,) + halves, F32),
            pltpu.VMEM((3,) + halves, F32),
            pltpu.VMEM((4,) + halves, F32),
            pltpu.VMEM((nz, 2) + halves, F32),
            pltpu.VMEM((PROJ, nt), F32),
            pltpu.VMEM((PROJ, nt), F32),
            pltpu.VMEM((nz, rows, LANES), F32),
            pltpu.VMEM((ndp, rows, LANES), F32),
            pltpu.VMEM((ndp, rows, LANES), F32),
            pltpu.VMEM((1, LANES), F32),
            pltpu.VMEM((ndp, 1, LANES), F32),
            pltpu.VMEM((1, LANES), F32),
            pltpu.VMEM((1, LANES), F32),
            dma((nz,)), dma((nz,)), dma((3,)),
            dma((nz,)), dma((nz,)), dma((6,)), dma((6,)), dma((6,)), dma((6,)),
            dma((6,)), dma((6,)), dma((6,)), dma((6,)), dma((nz,)), dma((nz,)),
            dma((ndp,)), dma((ndp,)), dma((ndp,)), dma((ndp,)), dma((ndp,)), dma((ndp,)),
            dma((ndp,)), dma((ndp,)), dma((2,)), pltpu.SemaphoreType.REGULAR,
        ],
        compiler_params=pltpu.CompilerParams(
            collective_id=0, has_side_effects=True, vmem_limit_bytes=24 * 2**20
        ),
        cost_estimate=pl.CostEstimate(
            flops=2 * tokens * (hidden + features) * PROJ,
            bytes_accessed=2 * tokens * (hidden + features),
            transcendentals=0,
        ),
    )(*in_hbm)
    raw = lax.dot_general(
        left, right, (((0,), (0,)), ((), ())),
        precision=lax.Precision.HIGHEST, preferred_element_type=F32,
    )
    return raw / scale[0, 0]


def solution(mesh):
    in_specs = (
        P("dp", "tensor"),
        P("dp", "tensor"),
        P("dp", None),
        P(None, "tensor"),
        P(None, "tensor"),
    )
    body = functools.partial(shards, mesh.shape["dp"], mesh.shape["tensor"] // 2)
    return jax.shard_map(
        body, mesh=mesh, in_specs=in_specs, out_specs=P("tensor", "dp"), check_vma=False
    )
```

time: 49.1 us -> 47.8 us (0.974)
  matrix products: 2.9 us -> 1.86 us
    dot_general x1, matrix products: 2.9 us -> 1.86 us  [shards(): lax.dot_general(left, right, (((0,), (0,)), ((), ())), precision=lax.Prec...]
where the time goes in v3:
time: 47.8 us; the launch traced here: 47.7 us
  Pallas kernels  45.9 us (96%)
  matrix products  1.86 us (4%)
    pallas_call x1, Pallas kernels, shards(): pl.pallas_call(functools.partial(kernel, ndp, nz, nt), out_shape=[jax.Sha...  45.9 us
    dot_general x1, matrix products, shards(): lax.dot_general(left, right, (((0,), (0,)), ((), ())), precision=lax.Prec...  1.86 us

profile of v3, /device:TPU:1, one launch (start us, length us, event | category | flops | bytes accessed | tf_op | source)
XLA Modules:
  0.0 47.7 jit_solution(5714043247009420651)
XLA Ops:
  0.0 45.9 %shard_map.55 = (f32[256,256]{1,0:T(8,128)S(1)}, f32[256,256]{1,0:T(8,128)S(1)}, f32[1,1]{1,0:T(1,128)}) custom-call(bf16[2048,1792]{1,0:T(8,128)(2,1)} %grad_hbm.1, bf16[2048,512]{1,0:T(8,128)(2,1)} %act_hbm.1, s32[1,2048]{1,0:T(1,128)} %seg_hbm.1, bf16[64,1792]{1,0:T(8,128)(2,1)} %po_hbm.1, bf16[64,512]{1,0:T(8,128)(2,1)} %pi_hbm.1), custom_call_target="tpu_custom_call" | custom-call | flops 603979776 | bytes 9437184 | tf_op jit(solution)/shard_map/pallas_call | solution.py:393
  45.9 1.9 %convolution_divide_fusion = f32[256,256]{1,0:T(8,128)} fusion(f32[256,256]{1,0:T(8,128)S(1)} %get-tuple-element.8, f32[256,256]{1,0:T(8,128)S(1)} %get-tuple-element.9, f32[]{:T(128)} %bitcast), kind=kOutput, calls=%fused_computation | convolution fusion | flops 201392128 | bytes 786436 | tf_op jit(solution)/shard_map/dot_general | solution.py:440

commit v4 on v3

--- a/solution.py
+++ b/solution.py
@@ -23,17 +23,17 @@
     return high, low
 
 
-def order(i):
-    return 4 - (i + 1) // 2 if i % 2 else 4 + i // 2
+ORDER = (4, 3, -3, 1, -1, 2, -2, 0)
+GROUPS = ((0, 1, 2), (3, 4), (5, 6), (7,))
 
 
 def kernel(
     ndp, nz, nt,
     grad_hbm, act_hbm, seg_hbm, po_hbm, pi_hbm, left_ref, right_ref, scale_ref,
-    gbuf, abuf, seg, wout, win, wt_out, wt_in, part, sib_recv, sums, far_recv, near_recv, tok,
-    high_ref, low_ref, xacc, rows, cols, ss, ss_all, ss_sum, ss_recv,
+    gbuf, abuf, seg, wout, win, wt_out, wt_in, part, sib_recv, sums, far_recv, last_recv, near_recv, tok,
+    high_ref, low_ref, xacc, message, rows, cols, ss_sum, ss_recv,
     g_sem, a_sem, w_sem, sib_s, sib_r, far_s, far_r, near_s, near_r, ag_s, ag_r, fa_s, fa_r,
-    sh_s, sh_r, row_s, row_r, col_s, col_r, fw_s, fw_r, sq_s, sq_r, ss_sem, ready,
+    sh_s, sh_r, row_s, row_r, col_s, col_r, fw_s, fw_r, ss_sem, ready,
 ):
     d = lax.axis_index("dp")
     t = lax.axis_index("tensor")
@@ -68,13 +68,14 @@
         copy.start()
     loads = []
     for i in range(nz):
-        first = pl.multiple_of(ring[order(i)] * chunk, chunk)
+        first = pl.multiple_of(ring[ORDER[i] % nz] * chunk, chunk)
         loads.append((
             pltpu.make_async_copy(grad_hbm.at[pl.ds(first, chunk)], gbuf.at[i], g_sem.at[i]),
             pltpu.make_async_copy(act_hbm.at[pl.ds(first, chunk)], abuf.at[i], a_sem.at[i]),
         ))
-        loads[-1][0].start()
-        loads[-1][1].start()
+    for i in GROUPS[0]:
+        loads[i][0].start()
+        loads[i][1].start()
 
     wout[pl.ds(PROJ, PROJ)] = jnp.zeros((PROJ, wout.shape[1]), BF16)
     win[pl.ds(0, PROJ)] = jnp.zeros((PROJ, win.shape[1]), BF16)
@@ -88,6 +89,10 @@
         for i in group:
             loads[i][0].wait()
             loads[i][1].wait()
+        if group == GROUPS[0]:
+            for i in range(len(group), nz):
+                loads[i][0].start()
+                loads[i][1].start()
         total = {}
         for source, weight in ((gbuf, wt_out), (abuf, wt_in)):
             for first in range(0, weight.shape[0], DEPTH):
@@ -100,8 +105,7 @@
         for i in group:
             part[i] = total[i].reshape((2, 2, nt // 2, LANES))
 
-    ahead = 3
-    project(range(ahead))
+    project(GROUPS[0])
     pl.semaphore_wait(barrier, len(greeted))
     for device in line:
         pl.semaphore_signal(ready, inc=1, device_id=device, device_id_type=MESH)
@@ -110,8 +114,9 @@
         remote(part.at[i, 1 - c], sib_recv.at[i], sib_s.at[i], sib_r.at[i], sibling)
         for i in range(nz)
     ]
-    at = {order(i) - nz if order(i) > 4 else order(i): i for i in range(nz)}
+    at = {offset: i for i, offset in enumerate(ORDER)}
     sides = (1, -1)
+    quarter = nt // 4
 
     def far(s, h):
         n = 2 * s + h
@@ -119,9 +124,11 @@
             sums.at[at[3 * sides[s]], h], far_recv.at[s, h], far_s.at[n], far_r.at[n], zdev(sides[s])
         )
 
-    def farthest(s):
-        return remote(
-            sums.at[at[4], s], far_recv.at[2, s], far_s.at[4 + s], far_r.at[4 + s], zdev(2 * sides[s])
+    def farthest(s, h):
+        n = 4 + 2 * s + h
+        return remote(
+            sums.at[at[4], h, pl.ds(s * quarter, quarter)], last_recv.at[s, h], far_s.at[n], far_r.at[n],
+            zdev(2 * sides[s]),
         )
 
     def near(s):
@@ -134,42 +141,28 @@
             zdev(2 * sides[s]),
         )
 
-    for i in range(ahead):
+    for i in GROUPS[0]:
         sib[i].start()
-    groups = {3: (3, 4), 5: (5, 6, 7)}
-    for i in range(nz):
-        if i in groups:
-            project(groups[i])
-            for later in groups[i]:
-                sib[later].start()
-        sib[i].wait_recv()
-        sums[i] = part[i, c] + sib_recv[i]
-        if i == at[4]:
-            farthest(0).start()
-            farthest(1).start()
-        for s in range(2):
-            if i == at[3 * sides[s]]:
-                far(s, 1 - s).start()
-                far(s, s).start()
-            if i == at[sides[s]]:
-                near(s).start()
-    for s in range(2):
-        far(s, 1 - s).wait_recv()
-        sums[at[2 * sides[s]], 1 - s] += far_recv[s, 1 - s]
-        second(s, 1 - s).start()
-    for s in range(2):
-        far(s, s).wait_recv()
-        farthest(s).wait_recv()
-        sums[at[2 * sides[s]], s] += far_recv[s, s] + far_recv[2, s]
-        second(s, s).start()
-    for s in range(2):
-        near(s).wait_recv()
-    tok[z, c] = sums[at[0]] + (near_recv[0] + near_recv[1])
-    for h in range(2):
-        second(0, h).wait_recv()
-        second(1, h).wait_recv()
-        tok[z, c, h] += near_recv[2, h] + near_recv[3, h]
-
+    for n, group in enumerate(GROUPS):
+        if 0 < n < len(GROUPS) - 1:
+            project(GROUPS[n + 1])
+            for i in GROUPS[n + 1]:
+                sib[i].start()
+        for i in group:
+            sib[i].wait_recv()
+            sums[i] = part[i, c] + sib_recv[i]
+            for s in range(2):
+                if i == at[sides[s]]:
+                    near(s).start()
+        if n == 0:
+            for h in range(2):
+                for s in range(2):
+                    farthest(s, h).start()
+                for s in range(2):
+                    far(s, h).start()
+            project(GROUPS[1])
+            for i in GROUPS[1]:
+                sib[i].start()
     def owner(k):
         return ring[k % nz]
 
@@ -185,13 +178,28 @@
         mine = tok.at[owner(-2 * sides[s]), c, h]
         return remote(mine, mine, fa_s.at[n], fa_r.at[n], zdev(sides[s]))
 
-    def opposite(s):
-        mine = tok.at[owner(-2 * sides[s]), c, s]
-        return remote(mine, mine, fa_s.at[4 + s], fa_r.at[4 + s], zdev(2 * sides[s]))
-
-    for first in range(2):
+    def opposite(s, h):
+        n = 4 + 2 * s + h
+        mine = tok.at[owner(-2 * sides[s]), c, h, pl.ds(s * quarter, quarter)]
+        return remote(mine, mine, fa_s.at[n], fa_r.at[n], zdev(2 * sides[s]))
+
+    for h in range(2):
         for s in range(2):
-            spread(s, s if first == 0 else 1 - s).start()
+            mine = pl.ds(s * quarter, quarter)
+            far(s, h).wait_recv()
+            sums[at[2 * sides[s]], h] += far_recv[s, h]
+            farthest(s, h).wait_recv()
+            sums[at[2 * sides[s]], h, mine] += last_recv[s, h]
+            second(s, h).start()
+    for s in range(2):
+        near(s).wait_recv()
+    for h in range(2):
+        beside_sums = sums[at[0], h] + (near_recv[0, h] + near_recv[1, h])
+        for s in range(2):
+            second(s, h).wait_recv()
+        tok[z, c, h] = beside_sums + (near_recv[2, h] + near_recv[3, h])
+        for s in range(2):
+            spread(s, h).start()
     for s in range(2):
         beside(s).start()
 
@@ -242,13 +250,12 @@
     share(0).start()
     own(0)
     others(0)
-    for s in range(2):
-        spread(s, s).wait_recv()
-        opposite(s).start()
-        onward(s, s).start()
-    for s in range(2):
-        spread(s, 1 - s).wait_recv()
-        onward(s, 1 - s).start()
+    for h in range(2):
+        for s in range(2):
+            spread(s, h).wait_recv()
+            opposite(s, h).start()
+            onward(s, h).start()
+    for s in range(2):
         share(-2 * sides[s]).start()
     for s in range(2):
         own(-2 * sides[s])
@@ -265,18 +272,20 @@
         for h in range(2):
             onward(s, h).wait_recv()
         share(-3 * sides[s]).start()
-    for s in range(2):
-        opposite(s).wait_recv()
+    own(-3 * sides[0])
+    for s in range(2):
+        for h in range(2):
+            opposite(s, h).wait_recv()
     share(4).start()
-    for s in range(2):
-        own(-3 * sides[s])
+    own(-3 * sides[1])
     own(4)
     for s in range(2):
         others(-3 * sides[s])
     others(4)
 
     squares = xacc[...] * xacc[...]
-    ss[...] = jnp.sum(squares.reshape(-1, LANES), axis=0, keepdims=True)
+    message[pl.ds(0, 2 * EXAMPLES)] = xacc[z]
+    message[pl.ds(2 * EXAMPLES, 1)] = jnp.sum(squares.reshape(-1, LANES), axis=0, keepdims=True)
     pl.semaphore_wait(ready, len(line))
 
     home = lax.div(d, 2)
@@ -295,17 +304,17 @@
     def forward(source):
         return remote(cols.at[source], cols.at[source], fw_s.at[source], fw_r.at[source], sibling)
 
+    sent = message.at[pl.ds(0, 2 * EXAMPLES + 1)]
+
     def row(k):
-        return remote(xacc.at[z], rows.at[d], row_s.at[k], row_r.at[d], (plane[k], t))
+        return remote(
+            sent, rows.at[d, pl.ds(0, 2 * EXAMPLES + 1)], row_s.at[k], row_r.at[d], (plane[k], t)
+        )
 
     def row_from(source):
-        return remote(xacc.at[z], rows.at[source], row_s.at[1], row_r.at[source], (source, t))
-
-    def square(k):
-        return remote(ss, ss_all.at[d], sq_s.at[k], sq_r.at[d], (plane[k], t))
-
-    def square_from(source):
-        return remote(ss, ss_all.at[source], sq_s.at[1], sq_r.at[source], (source, t))
+        return remote(
+            sent, rows.at[source, pl.ds(0, 2 * EXAMPLES + 1)], row_s.at[1], row_r.at[source], (source, t)
+        )
 
     for m in range(1, ndp // 2):
         column(m).start()
@@ -315,11 +324,8 @@
         column(0).start()
 
     for k in range(1, ndp):
-        square(k).start()
-    for k in range(1, ndp):
         row(k).start()
-    rows[d] = xacc[z]
-    ss_all[d] = ss[...]
+    rows[d, pl.ds(0, 2 * EXAMPLES + 1)] = message[pl.ds(0, 2 * EXAMPLES + 1)]
 
     @pl.when(forwards)
     def _():
@@ -331,12 +337,10 @@
             forward(source).start()
 
     for k in range(1, ndp):
-        square_from(plane[k]).wait_recv()
-    ss_sum[...] = jnp.sum(ss_all[...], axis=0)
+        row_from(plane[k]).wait_recv()
+    ss_sum[...] = jnp.sum(rows[:, pl.ds(2 * EXAMPLES, 1), :], axis=0)
     swap_ss = remote(ss_sum, ss_recv, ss_sem.at[0], ss_sem.at[1], sibling)
     swap_ss.start()
-    for k in range(1, ndp):
-        row_from(plane[k]).wait_recv()
 
     def matrix(ref, out):
         for jj in range(2):
@@ -359,16 +363,17 @@
     for copy in sib + [swap_ss] + [share(k) for k in range(nz)]:
         copy.wait_send()
     for s in range(2):
-        for copy in (farthest(s), near(s), beside(s), opposite(s)):
+        for copy in (near(s), beside(s)):
             copy.wait_send()
         for h in range(2):
-            for copy in (far(s, h), second(s, h), spread(s, h), onward(s, h)):
+            for copy in (
+                far(s, h), farthest(s, h), second(s, h), spread(s, h), onward(s, h), opposite(s, h)
+            ):
                 copy.wait_send()
     for m in range(1, ndp // 2):
         column(m).wait_send()
     for k in range(1, ndp):
         row(k).wait_send()
-        square(k).wait_send()
 
     @pl.when(forwards)
     def _():
@@ -410,23 +415,23 @@
             pltpu.VMEM((nz, 2) + halves, F32),
             pltpu.VMEM((nz,) + halves, F32),
             pltpu.VMEM((nz,) + halves, F32),
-            pltpu.VMEM((3,) + halves, F32),
+            pltpu.VMEM((2,) + halves, F32),
+            pltpu.VMEM((2, 2, nt // 4, LANES), F32),
             pltpu.VMEM((4,) + halves, F32),
             pltpu.VMEM((nz, 2) + halves, F32),
             pltpu.VMEM((PROJ, nt), F32),
             pltpu.VMEM((PROJ, nt), F32),
             pltpu.VMEM((nz, rows, LANES), F32),
+            pltpu.VMEM((rows + 8, LANES), F32),
+            pltpu.VMEM((ndp, rows + 8, LANES), F32),
             pltpu.VMEM((ndp, rows, LANES), F32),
-            pltpu.VMEM((ndp, rows, LANES), F32),
-            pltpu.VMEM((1, LANES), F32),
-            pltpu.VMEM((ndp, 1, LANES), F32),
             pltpu.VMEM((1, LANES), F32),
             pltpu.VMEM((1, LANES), F32),
             dma((nz,)), dma((nz,)), dma((3,)),
-            dma((nz,)), dma((nz,)), dma((6,)), dma((6,)), dma((6,)), dma((6,)),
-            dma((6,)), dma((6,)), dma((6,)), dma((6,)), dma((nz,)), dma((nz,)),
+            dma((nz,)), dma((nz,)), dma((8,)), dma((8,)), dma((6,)), dma((6,)),
+            dma((6,)), dma((6,)), dma((8,)), dma((8,)), dma((nz,)), dma((nz,)),
             dma((ndp,)), dma((ndp,)), dma((ndp,)), dma((ndp,)), dma((ndp,)), dma((ndp,)),
-            dma((ndp,)), dma((ndp,)), dma((2,)), pltpu.SemaphoreType.REGULAR,
+            dma((2,)), pltpu.SemaphoreType.REGULAR,
         ],
         compiler_params=pltpu.CompilerParams(
             collective_id=0, has_side_effects=True, vmem_limit_bytes=24 * 2**20

time: 47.8 us -> 45.1 us (0.944)
  Pallas kernels: 45.9 us -> 43.2 us
    pallas_call x1, Pallas kernels: 45.9 us -> 43.2 us  [shards(): pl.pallas_call(functools.partial(kernel, ndp, nz, nt), out_shape=[jax.Sha...]
where the time goes in v4:
time: 45.1 us; the launch traced here: 45 us
  Pallas kernels  43.2 us (96%)
  matrix products  1.86 us (4%)
    pallas_call x1, Pallas kernels, shards(): pl.pallas_call(functools.partial(kernel, ndp, nz, nt), out_shape=[jax.Sha...  43.2 us
    dot_general x1, matrix products, shards(): lax.dot_general(left, right, (((0,), (0,)), ((), ())), precision=lax.Prec...  1.86 us

profile of v4, /device:TPU:1, one launch (start us, length us, event | category | flops | bytes accessed | tf_op | source)
XLA Modules:
  0.0 45.0 jit_solution(7462648188612383142)
XLA Ops:
  0.0 43.2 %shard_map.55 = (f32[256,256]{1,0:T(8,128)S(1)}, f32[256,256]{1,0:T(8,128)S(1)}, f32[1,1]{1,0:T(1,128)}) custom-call(bf16[2048,1792]{1,0:T(8,128)(2,1)} %grad_hbm.1, bf16[2048,512]{1,0:T(8,128)(2,1)} %act_hbm.1, s32[1,2048]{1,0:T(1,128)} %seg_hbm.1, bf16[64,1792]{1,0:T(8,128)(2,1)} %po_hbm.1, bf16[64,512]{1,0:T(8,128)(2,1)} %pi_hbm.1), custom_call_target="tpu_custom_call" | custom-call | flops 603979776 | bytes 9437184 | tf_op jit(solution)/shard_map/pallas_call | solution.py:398
  43.2 1.9 %convolution_divide_fusion = f32[256,256]{1,0:T(8,128)} fusion(f32[256,256]{1,0:T(8,128)S(1)} %get-tuple-element.8, f32[256,256]{1,0:T(8,128)S(1)} %get-tuple-element.9, f32[]{:T(128)} %bitcast), kind=kOutput, calls=%fused_computation | convolution fusion | flops 201392128 | bytes 786436 | tf_op jit(solution)/shard_map/dot_general | solution.py:445

commit v5 on v4

--- a/solution.py
+++ b/solution.py
@@ -29,7 +29,7 @@
 
 def kernel(
     ndp, nz, nt,
-    grad_hbm, act_hbm, seg_hbm, po_hbm, pi_hbm, left_ref, right_ref, scale_ref,
+    grad_hbm, act_hbm, seg_hbm, po_hbm, pi_hbm, left_ref, right_ref,
     gbuf, abuf, seg, wout, win, wt_out, wt_in, part, sib_recv, sums, far_recv, last_recv, near_recv, tok,
     high_ref, low_ref, xacc, message, rows, cols, ss_sum, ss_recv,
     g_sem, a_sem, w_sem, sib_s, sib_r, far_s, far_r, near_s, near_r, ag_s, ag_r, fa_s, fa_r,
@@ -284,8 +284,10 @@
     others(4)
 
     squares = xacc[...] * xacc[...]
+    ss_sum[...] = jnp.sum(squares.reshape(-1, LANES), axis=0, keepdims=True)
+    swap_ss = remote(ss_sum, ss_recv, ss_sem.at[0], ss_sem.at[1], sibling)
+    swap_ss.start()
     message[pl.ds(0, 2 * EXAMPLES)] = xacc[z]
-    message[pl.ds(2 * EXAMPLES, 1)] = jnp.sum(squares.reshape(-1, LANES), axis=0, keepdims=True)
     pl.semaphore_wait(ready, len(line))
 
     home = lax.div(d, 2)
@@ -323,9 +325,18 @@
     def _():
         column(0).start()
 
+    swap_ss.wait_recv()
+    message[pl.ds(2 * EXAMPLES, 1)] = ss_sum[...] + ss_recv[...]
     for k in range(1, ndp):
         row(k).start()
     rows[d, pl.ds(0, 2 * EXAMPLES + 1)] = message[pl.ds(0, 2 * EXAMPLES + 1)]
+
+    def matrix(ref, jj):
+        return ref[:, pl.ds(jj * EXAMPLES, EXAMPLES), :].reshape(ndp * EXAMPLES, LANES)
+
+    def place_columns():
+        for jj in range(2):
+            right_ref[:, pl.ds(jj * LANES, LANES)] = matrix(cols, jj)
 
     @pl.when(forwards)
     def _():
@@ -335,30 +346,21 @@
             source = plane[k]
             column_from(source).wait_recv()
             forward(source).start()
+        place_columns()
 
     for k in range(1, ndp):
         row_from(plane[k]).wait_recv()
-    ss_sum[...] = jnp.sum(rows[:, pl.ds(2 * EXAMPLES, 1), :], axis=0)
-    swap_ss = remote(ss_sum, ss_recv, ss_sem.at[0], ss_sem.at[1], sibling)
-    swap_ss.start()
-
-    def matrix(ref, out):
-        for jj in range(2):
-            out[:, pl.ds(jj * LANES, LANES)] = ref[:, pl.ds(jj * EXAMPLES, EXAMPLES), :].reshape(
-                ndp * EXAMPLES, LANES
-            )
-
-    matrix(rows, left_ref)
+    trace = jnp.sum(rows[:, pl.ds(2 * EXAMPLES, 1), :], axis=0)
+    trace = jnp.sum(trace, axis=1, keepdims=True)
+    scale = 1.0 / (trace / (PROJ * PROJ) + 1e-6)
+    for jj in range(2):
+        left_ref[:, pl.ds(jj * LANES, LANES)] = matrix(rows, jj) * scale
 
     @pl.when(jnp.logical_not(forwards))
     def _():
         for k in range(ndp):
             forward(plane[k]).wait_recv()
-
-    matrix(cols, right_ref)
-    swap_ss.wait_recv()
-    trace = jnp.sum(ss_sum[...] + ss_recv[...], keepdims=True)
-    scale_ref[...] = trace / (PROJ * PROJ) + 1e-6
+        place_columns()
 
     for copy in sib + [swap_ss] + [share(k) for k in range(nz)]:
         copy.wait_send()
@@ -395,15 +397,14 @@
     halves = (2, nt // 2, LANES)
     arrays = (grad_up, activations, segment_ids, proj_out, proj_in)
     in_hbm = [pltpu.with_memory_space_constraint(array, pltpu.HBM) for array in arrays]
-    left, right, scale = pl.pallas_call(
+    left, right = pl.pallas_call(
         functools.partial(kernel, ndp, nz, nt),
         out_shape=[
             jax.ShapeDtypeStruct((ndp * EXAMPLES, block), F32),
             jax.ShapeDtypeStruct((ndp * EXAMPLES, block), F32),
-            jax.ShapeDtypeStruct((1, 1), F32),
         ],
         in_specs=[pl.BlockSpec(memory_space=pltpu.HBM)] * 5,
-        out_specs=[pl.BlockSpec(memory_space=pltpu.VMEM)] * 3,
+        out_specs=[pl.BlockSpec(memory_space=pltpu.VMEM)] * 2,
         scratch_shapes=[
             pltpu.VMEM((nz, 2 * nt, hidden), BF16),
             pltpu.VMEM((nz, 2 * nt, features), BF16),
@@ -442,11 +443,10 @@
             transcendentals=0,
         ),
     )(*in_hbm)
-    raw = lax.dot_general(
+    return lax.dot_general(
         left, right, (((0,), (0,)), ((), ())),
-        precision=lax.Precision.HIGHEST, preferred_element_type=F32,
+        precision=lax.Precision.HIGH, preferred_element_type=F32,
     )
-    return raw / scale[0, 0]
 
 
 def solution(mesh):

time: 45.1 us -> 42.1 us (0.933)
  Pallas kernels: 43.2 us -> 40.9 us
  matrix products: 1.86 us -> 1.09 us
    pallas_call x1, Pallas kernels: 43.2 us -> 40.9 us  [shards(): pl.pallas_call(functools.partial(kernel, ndp, nz, nt), out_shape=[jax.Sha...]
    dot_general x1, matrix products: 1.86 us -> 1.09 us  [shards(): lax.dot_general(left, right, (((0,), (0,)), ((), ())), precision=lax.Prec...]
where the time goes in v5:
time: 42.1 us; the launch traced here: 42 us
  Pallas kernels  40.9 us (97%)
  matrix products  1.09 us (3%)
    pallas_call x1, Pallas kernels, shards(): pl.pallas_call(functools.partial(kernel, ndp, nz, nt), out_shape=[jax.Sha...  40.9 us
    dot_general x1, matrix products, shards(): lax.dot_general(left, right, (((0,), (0,)), ((), ())), precision=lax.Prec...  1.09 us

profile of v5, /device:TPU:1, one launch (start us, length us, event | category | flops | bytes accessed | tf_op | source)
XLA Modules:
  0.0 42.0 jit_solution(5319123475210277379)
XLA Ops:
  0.0 40.9 %shard_map.55 = (f32[256,256]{1,0:T(8,128)S(1)}, f32[256,256]{1,0:T(8,128)S(1)}) custom-call(bf16[2048,1792]{1,0:T(8,128)(2,1)} %grad_hbm.1, bf16[2048,512]{1,0:T(8,128)(2,1)} %act_hbm.1, s32[1,2048]{1,0:T(1,128)} %seg_hbm.1, bf16[64,1792]{1,0:T(8,128)(2,1)} %po_hbm.1, bf16[64,512]{1,0:T(8,128)(2,1)} %pi_hbm.1), custom_call_target="tpu_custom_call" | custom-call | flops 603979776 | bytes 9437184 | tf_op jit(solution)/shard_map/pallas_call | solution.py:400
  40.9 1.1 %fusion = f32[256,256]{1,0:T(8,128)} fusion(f32[256,256]{1,0:T(8,128)S(1)} %get-tuple-element.7, f32[256,256]{1,0:T(8,128)S(1)} %get-tuple-element.8), kind=kOutput, calls=%fused_computation | convolution fusion | flops 100663296 | bytes 786432 | tf_op jit(solution)/shard_map/dot_general | solution.py:446

commit v6 on v5

--- a/solution.py
+++ b/solution.py
@@ -253,8 +253,8 @@
     for h in range(2):
         for s in range(2):
             spread(s, h).wait_recv()
+            onward(s, h).start()
             opposite(s, h).start()
-            onward(s, h).start()
     for s in range(2):
         share(-2 * sides[s]).start()
     for s in range(2):

time: 42.1 us -> 41.8 us (level)
  no operation moved by 1% of the time
where the time goes in v6:
time: 41.8 us; the launch traced here: 41.7 us
  Pallas kernels  40.6 us (97%)
  matrix products  1.09 us (3%)
    pallas_call x1, Pallas kernels, shards(): pl.pallas_call(functools.partial(kernel, ndp, nz, nt), out_shape=[jax.Sha...  40.6 us
    dot_general x1, matrix products, shards(): lax.dot_general(left, right, (((0,), (0,)), ((), ())), precision=lax.Prec...  1.09 us

profile of v6, /device:TPU:1, one launch (start us, length us, event | category | flops | bytes accessed | tf_op | source)
XLA Modules:
  0.0 41.7 jit_solution(11932550671846930688)
XLA Ops:
  0.0 40.6 %shard_map.55 = (f32[256,256]{1,0:T(8,128)S(1)}, f32[256,256]{1,0:T(8,128)S(1)}) custom-call(bf16[2048,1792]{1,0:T(8,128)(2,1)} %grad_hbm.1, bf16[2048,512]{1,0:T(8,128)(2,1)} %act_hbm.1, s32[1,2048]{1,0:T(1,128)} %seg_hbm.1, bf16[64,1792]{1,0:T(8,128)(2,1)} %po_hbm.1, bf16[64,512]{1,0:T(8,128)(2,1)} %pi_hbm.1), custom_call_target="tpu_custom_call" | custom-call | flops 603979776 | bytes 9437184 | tf_op jit(solution)/shard_map/pallas_call | solution.py:400
  40.6 1.1 %fusion = f32[256,256]{1,0:T(8,128)} fusion(f32[256,256]{1,0:T(8,128)S(1)} %get-tuple-element.7, f32[256,256]{1,0:T(8,128)S(1)} %get-tuple-element.8), kind=kOutput, calls=%fused_computation | convolution fusion | flops 100663296 | bytes 786432 | tf_op jit(solution)/shard_map/dot_general | solution.py:446
